TPU v7x, 512 devices: a whole 4x4x16 slice. The times are simulated.
512 devices in a mesh: mode: 16 (over x, z_hi), mer: 32 (over y, z_lo, core).
Axes of the slice: x: 4, y: 4, z: 16 (z_hi: 4, z_lo: 4; z = z_hi * 4 + z_lo), core: 2. Of those that a mesh axis runs over, the one named last changes fastest.
Arguments:
- mode_fields: bfloat16 [12, 128, 2, 65536], P(None, 'mode', None, 'mer'), may hold values from -0.5 to 0.5
- radius: float32 [65536], P('mer'), may hold values from 1 to 4
- radial_blocks: bfloat16 [5, 64, 65536], P(None, None, 'mer'), may hold values from -6 to 6
- axial_blocks: bfloat16 [5, 64, 65536], P(None, None, 'mer'), may hold values from -6 to 6
- block_columns: int32 [1024, 5], P('mer'), may hold values from 0 to 39, as said below
- interface_nodes: int32 [64, 256], P('mer'), may hold values from 0 to 2047, as said below
Outputs:
- induction: float32 [3, 128, 2, 65536], P(None, 'mode', None, 'mer')
- momentum: float32 [3, 128, 2, 65536], P(None, 'mode', None, 'mer')
Inputs may be any that keep to these rules, and one draw needn't show every extreme that they name: `block_columns`: indices into the extended list of a subdomain's block row: its 2048 nodes, then the 256 nodes received from the previous subdomain, then the 256 from the next, counted in blocks of 64. `interface_nodes`: row 2 d lists the local nodes subdomain d sends to subdomain d - 1, row 2 d + 1 those it sends to d + 1; each row holds 256 distinct local node indices.
All inputs are finite; a program needn't handle non-finite values.
Results may differ from a plain program's by a relative error of at most 0.0057.
Values may be sent and summed in bfloat16 or wider, within the bound.
A program may use at most 64 MiB of HBM per device.

v0:
```python
import math

import jax
import jax.numpy as jnp
from jax import lax
from jax.sharding import PartitionSpec as P

M = 128
THETA = 256
BLK = 64
NNZB = 5


def from_behind(value, axis, steps):
    count = lax.axis_size(axis)
    initial, last = (max(0, -steps), min(count, count - steps))
    return lax.ppermute(value, axis, [(source, source + steps) for source in range(initial, last)])


def tables(mode_total, angle_total):
    mode_ids = jnp.arange(mode_total, dtype=jnp.int32)
    angle_ids = jnp.arange(angle_total, dtype=jnp.int32)
    phase = angle_ids[:, None] * mode_ids[None, :] % angle_total
    angle = phase.astype(jnp.float32) * (2.0 * math.pi / angle_total)
    weight = jnp.where(mode_ids == 0, 1.0, 2.0).astype(jnp.float32)
    cosines = jnp.cos(angle)
    sines = jnp.sin(angle)
    inverse = jnp.stack([weight * cosines, -weight * sines], axis=-1).astype(jnp.bfloat16)
    forward = (jnp.stack([cosines.T, -sines.T], axis=1) / angle_total).astype(jnp.bfloat16)
    return (inverse, forward)


def cross_product(first, second):
    return jnp.stack(
        [
            first[1] * second[2] - first[2] * second[1],
            first[2] * second[0] - first[0] * second[2],
            first[0] * second[1] - first[1] * second[0],
        ]
    )


def nonlinear(received, inverse, forward):
    physical = jnp.einsum("tmp,cmpn->ctn", inverse, received, preferred_element_type=jnp.float32)
    velocity = physical[0:3]
    magnetic = physical[3:6]
    current = physical[6:9]
    vorticity = physical[9:12]
    energy = 0.5 * jnp.sum(velocity * velocity, axis=0, keepdims=True)
    lorentz = cross_product(current, magnetic) + cross_product(velocity, vorticity)
    products = jnp.concatenate([cross_product(velocity, magnetic), energy, lorentz], axis=0).astype(
        jnp.bfloat16
    )
    return jnp.einsum(
        "mpt,ctn->cmpn", forward, products, preferred_element_type=jnp.float32
    ).astype(jnp.bfloat16)


def rotated(values, mode_values):
    return jnp.stack(
        [-mode_values[:, None] * values[:, 1], mode_values[:, None] * values[:, 0]], axis=1
    )


def derive(extended, local, radial_part, axial_part, columns, radius, mode_values):
    mode_count = local.shape[1]
    node_count = local.shape[3]
    block_count = node_count // BLK
    vectors = extended.reshape(4 * mode_count * 2, extended.shape[3] // BLK, BLK)
    picked = vectors[:, columns]
    radial_four = radial_part.reshape(NNZB, BLK, block_count, BLK)
    axial_four = axial_part.reshape(NNZB, BLK, block_count, BLK)
    along_r = jnp.einsum(
        "vbkc,kcbr->vbr", picked, radial_four, preferred_element_type=jnp.float32
    ).reshape(4, mode_count, 2, node_count)
    along_z = jnp.einsum(
        "vbkc,kcbr->vbr", picked, axial_four, preferred_element_type=jnp.float32
    ).reshape(4, mode_count, 2, node_count)
    values = local.astype(jnp.float32)
    inv_radius = 1.0 / radius
    induction = jnp.stack(
        [
            rotated(values[2], mode_values) * inv_radius - along_z[1],
            along_z[0] - along_r[2],
            along_r[1] + values[1] * inv_radius - rotated(values[0], mode_values) * inv_radius,
        ]
    )
    momentum = jnp.stack(
        [
            values[4] - along_r[3],
            values[5] - rotated(values[3], mode_values) * inv_radius,
            values[6] - along_z[3],
        ]
    )
    return (induction, momentum)


def body(mode_fields, radius, radial_blocks, axial_blocks, block_columns, interface_nodes):
    mode_count = mode_fields.shape[1]
    share_count = lax.axis_size("mode")
    mode_values = (
        lax.axis_index("mode") * mode_count + jnp.arange(mode_count, dtype=jnp.int32)
    ).astype(jnp.float32)
    inverse, forward = tables(M, THETA)
    width = mode_fields.shape[3]
    divided = mode_fields.reshape(12, mode_count, 2, share_count, width // share_count)
    received = lax.all_to_all(divided, "mode", split_axis=3, concat_axis=1, tiled=True)
    layout = received.shape
    flattened = received.reshape(12, layout[1], 2, layout[3] * layout[4])
    terms = nonlinear(flattened, inverse, forward).reshape(7, layout[1], 2, layout[3], layout[4])
    returned = lax.all_to_all(terms, "mode", split_axis=1, concat_axis=3, tiled=True)
    local = returned.reshape(7, mode_count, 2, width)
    data = local[0:4]
    toward_next = data[..., interface_nodes[1]]
    toward_prev = data[..., interface_nodes[0]]
    from_prev = from_behind(toward_next, "mer", 1)
    from_next = from_behind(toward_prev, "mer", -1)
    extended = jnp.concatenate([data, from_prev, from_next], axis=3)
    return derive(extended, local, radial_blocks, axial_blocks, block_columns, radius, mode_values)


def solution(mesh):
    placed = (
        P(None, "mode", None, "mer"),
        P("mer"),
        P(None, None, "mer"),
        P(None, None, "mer"),
        P("mer", None),
        P("mer", None),
    )
    return jax.shard_map(
        body,
        mesh=mesh,
        in_specs=placed,
        out_specs=(P(None, "mode", None, "mer"), P(None, "mode", None, "mer")),
        check_vma=False,
    )
```

profile of v0, /device:TPU:26, one launch (start us, length us, event | category | flops | bytes accessed | tf_op | source)
XLA Modules:
  0.0 142.1 jit_solution(5692029764140418546)
XLA Ops:
  0.6 2.4 %reshape.509 = bf16[12,8,2,16,128]{4,3,2,1,0:T(8,128)(2,1)S(1)} reshape(bf16[12,8,2,2048]{3,2,1,0:T(2,128)(2,1)} %param.6) | data formatting | bytes 1572864 | tf_op jit(solution)/shard_map/reshape | solution.py:106
  3.1 1.2 copy.100
  4.3 18.1 %all-to-all-start = ((bf16[12,8,2,16,128]{4,1,2,0,3:T(8,128)(2,1)}), bf16[12,8,2,16,128]{4,1,2,0,3:T(8,128)(2,1)S(1)}, u32[]{:S(2)}, u32[]{:S(2)}) async-start(bf16[12,8,2,16,128]{4,1,2,0,3:T(8,128)(2,1)} %copy.100), calls=%async_computation | async-start | bytes 1572864 | tf_op jit(solution)/shard_map/all_to_all | solution.py:107
  22.4 0.5 sine_negate_fusion
  22.9 0.5 multiply_convert_fusion.1
  23.5 41.9 %all-to-all-done = bf16[12,8,2,16,128]{4,1,2,0,3:T(8,128)(2,1)S(1)} async-done(((bf16[12,8,2,16,128]{4,1,2,0,3:T(8,128)(2,1)}), bf16[12,8,2,16,128]{4,1,2,0,3:T(8,128)(2,1)S(1)}, u32[]{:S(2)}, u32[]{:S(2)}) %all-to-all-start) | async-done | bytes 786464 | tf_op jit(solution)/shard_map/all_to_all | solution.py:107
  65.4 0.4 convolution_bitcast_fusion
  66.2 0.3 fusion.10
  66.5 1.4 copy.103
  67.9 6.2 %all-to-all-start.1 = ((bf16[7,128,2,1,128]{4,2,0,3,1:T(2,128)(2,1)}), bf16[7,128,2,1,128]{4,2,0,3,1:T(2,128)(2,1)S(1)}, u32[]{:S(2)}, u32[]{:S(2)}) async-start(bf16[7,128,2,1,128]{4,2,0,3,1:T(2,128)(2,1)} %copy.103), calls=%async_computation.1 | async-start | bytes 917504 | tf_op jit(solution)/shard_map/all_to_all | solution.py:111
  74.3 3.9 %reshape.475 = bf16[5,64,32,64]{3,2,1,0:T(8,128)(2,1)} reshape(bf16[5,64,2048]{2,1,0:T(8,128)(2,1)S(1)} %copy-done.1) | data formatting | bytes 2621440 | tf_op jit(solution)/shard_map/reshape | solution.py:72
  78.2 3.8 %reshape.476 = bf16[5,64,32,64]{3,2,1,0:T(8,128)(2,1)} reshape(bf16[5,64,2048]{2,1,0:T(8,128)(2,1)S(1)} %copy-done.2) | data formatting | bytes 2621440 | tf_op jit(solution)/shard_map/reshape | solution.py:71
  82.0 0.5 fusion.54
  82.6 19.5 %all-to-all-done.1 = bf16[7,128,2,1,128]{4,2,0,3,1:T(2,128)(2,1)S(1)} async-done(((bf16[7,128,2,1,128]{4,2,0,3,1:T(2,128)(2,1)}), bf16[7,128,2,1,128]{4,2,0,3,1:T(2,128)(2,1)S(1)}, u32[]{:S(2)}, u32[]{:S(2)}) %all-to-all-start.1) | async-done | bytes 458784 | tf_op jit(solution)/shard_map/all_to_all | solution.py:111
  102.3 4.6 %copy.105 = bf16[4,8,2,2048]{1,0,3,2:T(4,128)(2,1)} copy(bf16[4,8,2,2048]{3,1,2,0:T(8,128)(2,1)S(1)} %slice_bitcast_fusion) | data formatting | bytes 524288 | tf_op jit(solution)/shard_map/slice | solution.py:113
  106.9 3.4 %gather_fusion.1 = bf16[256,4,8,2]{2,1,3,0:T(4,128)(2,1)S(1)} fusion(bf16[4,8,2,2048]{1,0,3,2:T(4,128)(2,1)} %copy.105, s32[1024]{0:T(1024)S(1)} %get-tuple-element.48), kind=kCustom, calls=%fused_computation.1 | custom fusion | bytes 66560 | tf_op jit(solution)/shard_map/gather | solution.py:115
  110.3 1.9 %collective-permute-start.1 = (bf16[4,8,2,256]{1,0,2,3:T(4,128)(2,1)S(1)}, bf16[4,8,2,256]{1,0,2,3:T(4,128)(2,1)S(1)}, u32[]{:S(2)}, u32[]{:S(2)}) collective-permute-start(bf16[4,8,2,256]{1,0,2,3:T(4,128)(2,1)S(1)} %bitcast.94), channel_id=1, source_target_pairs={{1,0},{2,1},{3,2},{4,3},{5,4},{6,5},{7,6},{8,7},{9,8},{10,9},{11,1... | collective-permute-start | bytes 98312 | tf_op jit(solution)/shard_map/ppermute | solution.py:17
  112.2 3.4 %gather_fusion = bf16[256,4,8,2]{2,1,3,0:T(4,128)(2,1)S(1)} fusion(bf16[4,8,2,2048]{1,0,3,2:T(4,128)(2,1)} %copy.105, s32[1024]{0:T(1024)S(1)} %pad_clamp_fusion.2), kind=kCustom, calls=%fused_computation | custom fusion | bytes 66560 | tf_op jit(solution)/shard_map/gather | solution.py:114
  115.7 2.6 %collective-permute-start = (bf16[4,8,2,256]{1,0,2,3:T(4,128)(2,1)S(1)}, bf16[4,8,2,256]{1,0,2,3:T(4,128)(2,1)S(1)}, u32[]{:S(2)}, u32[]{:S(2)}) collective-permute-start(bf16[4,8,2,256]{1,0,2,3:T(4,128)(2,1)S(1)} %bitcast.95), channel_id=1, source_target_pairs={{0,1},{1,2},{2,3},{3,4},{4,5},{5,6},{6,7},{7,8},{8,9},{9,10},{10,1... | collective-permute-start | bytes 98312 | tf_op jit(solution)/shard_map/ppermute | solution.py:17
  118.3 1.5 %fusion.46 = (f32[1,8,1,2048]{3,1,2,0:T(8,128)}, f32[1,8,1,2048]{3,1,2,0:T(8,128)}, f32[1,8,1,2048]{3,1,2,0:T(8,128)}, f32[1,8,1,2048]{3,1,2,0:T(8,128)}, f32[1,...) fusion(f32[8,2,2048]{2,0,1:T(8,128)S(1)} %get-tuple-element.23, f32[8]{0:T(128)} %fusion.54, f32[8]{0:T(128)S(1)} %add_convert_fusion, ...), kind=kLoop, calls=%fused_computation.89 | loop fusion | flops 98304 | bytes 786496 | tf_op jit(solution)/shard_map/stack | solution.py:60
  119.8 0.7 copy.122
  120.5 0.7 copy.128
  121.3 0.3 copy.108
  121.6 7.3 %collective-permute-done = bf16[4,8,2,256]{1,0,2,3:T(4,128)(2,1)S(1)} collective-permute-done((bf16[4,8,2,256]{1,0,2,3:T(4,128)(2,1)S(1)}, bf16[4,8,2,256]{1,0,2,3:T(4,128)(2,1)S(1)}, u32[]{:S(2)}, u32[]{:S(2)}) %collective-permute-start) | collective-permute-done | bytes 32800 | tf_op jit(solution)/shard_map/ppermute | solution.py:17
  128.9 0.3 copy.107
  129.5 0.4 reshape.474
  130.0 1.1 gather_fusion.2
  131.1 4.2 %fusion.4 = f32[64,32,64]{2,0,1:T(8,128)S(1)} fusion(bf16[64,32,5,64]{3,0,2,1:T(8,128)(2,1)S(1)} %bitcast.86, bf16[5,64,32,64]{3,2,1,0:T(8,128)(2,1)} %reshape.475), kind=kOutput, calls=%fused_computation.8 | convolution fusion | flops 83886080 | bytes 3145728 | tf_op jit(solution)/shard_map/vbkc,kcbr->vbr/dot_general | solution.py:76
  135.4 2.3 %fusion.7 = f32[64,32,64]{2,0,1:T(8,128)S(1)} fusion(bf16[64,32,5,64]{3,0,2,1:T(8,128)(2,1)S(1)} %bitcast.87, bf16[5,64,32,64]{3,2,1,0:T(8,128)(2,1)S(1)} %copy-done), kind=kOutput, calls=%fused_computation.9 | convolution fusion | flops 83886080 | bytes 3145728 | tf_op jit(solution)/shard_map/vbkc,kcbr->vbr/dot_general | solution.py:73
  139.3 0.3 fusion.30
  139.7 1.1 copy.133
  141.1 1.1 copy.132
  (71 shorter events, 3.1 us)
Async XLA Ops:
  4.3 61.1 %all-to-all-start = ((bf16[12,8,2,16,128]{4,1,2,0,3:T(8,128)(2,1)}), bf16[12,8,2,16,128]{4,1,2,0,3:T(8,128)(2,1)S(1)}, u32[]{:S(2)}, u32[]{:S(2)}) async-start(bf16[12,8,2,16,128]{4,1,2,0,3:T(8,128)(2,1)} %copy.100), calls=%async_computation | async-start | bytes 1572864 | tf_op jit(solution)/shard_map/all_to_all | solution.py:107
  66.0 8.1 %copy-start.12 = (s32[32,5]{0,1:T(8,128)S(1)}, s32[32,5]{0,1:T(8,128)}, u32[]{:S(2)}) copy-start(s32[32,5]{0,1:T(8,128)} %param.10) | copy-start | bytes 1924
  66.0 8.3 %copy-start.1 = (bf16[5,64,2048]{2,1,0:T(8,128)(2,1)S(1)}, bf16[5,64,2048]{2,1,0:T(8,128)(2,1)}, u32[]{:S(2)}) copy-start(bf16[5,64,2048]{2,1,0:T(8,128)(2,1)} %param.9) | copy-start | bytes 3932164
  67.9 10.3 %copy-start.2 = (bf16[5,64,2048]{2,1,0:T(8,128)(2,1)S(1)}, bf16[5,64,2048]{2,1,0:T(8,128)(2,1)}, u32[]{:S(2)}) copy-start(bf16[5,64,2048]{2,1,0:T(8,128)(2,1)} %param.8) | copy-start | bytes 3932164
  67.9 34.2 %all-to-all-start.1 = ((bf16[7,128,2,1,128]{4,2,0,3,1:T(2,128)(2,1)}), bf16[7,128,2,1,128]{4,2,0,3,1:T(2,128)(2,1)S(1)}, u32[]{:S(2)}, u32[]{:S(2)}) async-start(bf16[7,128,2,1,128]{4,2,0,3,1:T(2,128)(2,1)} %copy.103), calls=%async_computation.1 | async-start | bytes 917504 | tf_op jit(solution)/shard_map/all_to_all | solution.py:111
  78.2 4.3 %copy-start.13 = (s32[2,256]{1,0:T(2,128)S(1)}, s32[2,256]{1,0:T(2,128)}, u32[]{:S(2)}) copy-start(s32[2,256]{1,0:T(2,128)} %param.11) | copy-start | bytes 6148
  78.2 4.4 %copy-start.11 = (f32[2048]{0:T(1024)S(1)}, f32[2048]{0:T(1024)}, u32[]{:S(2)}) copy-start(f32[2048]{0:T(1024)} %param.7) | copy-start | bytes 24580
  110.3 11.0 %collective-permute-start.1 = (bf16[4,8,2,256]{1,0,2,3:T(4,128)(2,1)S(1)}, bf16[4,8,2,256]{1,0,2,3:T(4,128)(2,1)S(1)}, u32[]{:S(2)}, u32[]{:S(2)}) collective-permute-start(bf16[4,8,2,256]{1,0,2,3:T(4,128)(2,1)S(1)} %bitcast.94), channel_id=1, source_target_pairs={{1,0},{2,1},{3,2},{4,3},{5,4},{6,5},{7,6},{8,7},{9,8},{10,9},{11,1... | collective-permute-start | bytes 98312 | tf_op jit(solution)/shard_map/ppermute | solution.py:17
  115.7 13.2 %collective-permute-start = (bf16[4,8,2,256]{1,0,2,3:T(4,128)(2,1)S(1)}, bf16[4,8,2,256]{1,0,2,3:T(4,128)(2,1)S(1)}, u32[]{:S(2)}, u32[]{:S(2)}) collective-permute-start(bf16[4,8,2,256]{1,0,2,3:T(4,128)(2,1)S(1)} %bitcast.95), channel_id=1, source_target_pairs={{0,1},{1,2},{2,3},{3,4},{4,5},{5,6},{6,7},{7,8},{8,9},{9,10},{10,1... | collective-permute-start | bytes 98312 | tf_op jit(solution)/shard_map/ppermute | solution.py:17
  131.1 4.3 %copy-start = (bf16[5,64,32,64]{3,2,1,0:T(8,128)(2,1)S(1)}, bf16[5,64,32,64]{3,2,1,0:T(8,128)(2,1)}, u32[]{:S(2)}) copy-start(bf16[5,64,32,64]{3,2,1,0:T(8,128)(2,1)} %reshape.476) | copy-start | bytes 3932164
  137.7 1.2 copy-start.4
  137.9 1.2 copy-start.3
  137.9 1.4 copy-start.5
  137.9 1.4 copy-start.6
  137.9 1.4 copy-start.7
  137.9 1.4 copy-start.8
  137.9 1.4 copy-start.9
  137.9 1.4 copy-start.10
where the time goes:
time: 143 us; the launch traced here: 142 us
  waiting for transfers between devices  68.7 us (48%)
  local copies, waits for them, and re-layouts  31.7 us (22%)
  starting transfers between devices  28.8 us (20%)
  matrix products  7.29 us (5%)
  other arithmetic  4.44 us (3%)
    all_to_all x1, waiting for transfers between devices, body(): lax.all_to_all(divided, 'mode', split_axis=3, concat_axis=1, tiled=True)  41.9 us
    all_to_all x1, waiting for transfers between devices, body(): lax.all_to_all(terms, 'mode', split_axis=1, concat_axis=3, tiled=True)  19.5 us
    all_to_all x1, starting transfers between devices, body(): lax.all_to_all(divided, 'mode', split_axis=3, concat_axis=1, tiled=True)  18.1 us
    ppermute x2, waiting for transfers between devices, from_behind(): lax.ppermute(value, axis, [(source, source + steps) for source in range(i...  7.3 us
    all_to_all x1, starting transfers between devices, body(): lax.all_to_all(terms, 'mode', split_axis=1, concat_axis=3, tiled=True)  6.23 us
    slice x2, local copies, waits for them, and re-layouts, body(): data = local[0:4]  4.58 us
    ppermute x2, starting transfers between devices, from_behind(): lax.ppermute(value, axis, [(source, source + steps) for source in range(i...  4.51 us
    dot_general x1, matrix products, derive(): jnp.einsum('vbkc,kcbr->vbr', picked, axial_four, preferred_element_type=j...  4.23 us
  transfers between devices with their start and end apart: 4, of which 3 were waited for; matrix products, arithmetic and copies ran while one was open for 11% of the time, Pallas kernels for 0%

commit v1 on v0

v1 whole, which is shorter than its diff:
```python
import functools
import math

import jax
import jax.numpy as jnp
import numpy as np
from jax import lax
from jax.experimental import pallas as pl
from jax.experimental.pallas import tpu as pltpu
from jax.sharding import PartitionSpec as P

M = 128
THETA = 256
BLK = 64
NNZB = 5
MESH = pl.DeviceIdType.MESH
PEERS = [(dx, dz) for dz in (2, 1, 3, 0) for dx in (0, 1, 2, 3) if (dx, dz) != (0, 0)]
ROWS = 16
HALF = ROWS // 2
NODES = 2048
HALO = 256
EXT = NODES + 2 * HALO
TILE = 128
DEPTH = 384


def tables():
    modes = np.arange(M, dtype=np.int32)
    angles = np.arange(THETA, dtype=np.int32)
    phase = (angles[:, None] * modes[None, :]) % THETA
    angle = phase.astype(np.float32) * np.float32(2.0 * math.pi / THETA)
    weight = np.where(modes == 0, 1.0, 2.0).astype(np.float32)
    cosines, sines = np.cos(angle), np.sin(angle)
    inverse = np.stack([weight * cosines, -weight * sines], axis=-1).reshape(THETA, 2 * M)
    forward = np.stack([cosines.T, -sines.T], axis=0) / np.float32(THETA)
    forward = forward.reshape(2, 16, M // 16, THETA).transpose(1, 0, 2, 3).reshape(2 * M, THETA)
    return jnp.asarray(inverse.astype(jnp.bfloat16)), jnp.asarray(forward.astype(jnp.bfloat16))


def dot(a, b):
    return jnp.dot(a, b, preferred_element_type=jnp.float32)


def exchange(
    x, inv, fwd, nodes, out_ext, out_lor,
    recv, phys, prod, send, ext, lor, gath, halo, invv, fwdv, nodev,
    lsem, osem, s1, r1, s2, r2, sh, rh,
):
    me, dom = lax.axis_index("mode"), lax.axis_index("mer")
    doms = lax.axis_size("mer")
    mx, mz = me // 4, me % 4
    peers = [lax.rem(mx + dx, 4) * 4 + lax.rem(mz + dz, 4) for dx, dz in PEERS]
    has_prev, has_next = dom > 0, dom < doms - 1

    bar = pltpu.get_barrier_semaphore()
    for t in peers:
        pl.semaphore_signal(bar, inc=1, device_id={"mode": t}, device_id_type=MESH)

    @pl.when(has_prev)
    def _():
        pl.semaphore_signal(bar, inc=1, device_id={"mer": dom - 1}, device_id_type=MESH)

    @pl.when(has_next)
    def _():
        pl.semaphore_signal(bar, inc=1, device_id={"mer": dom + 1}, device_id_type=MESH)

    def columns(t):
        return pl.ds(pl.multiple_of(t * TILE, TILE), TILE)

    def rows(t):
        return pl.ds(pl.multiple_of(t * ROWS, ROWS), ROWS)

    loads = [
        pltpu.make_async_copy(a, b, lsem.at[i])
        for i, (a, b) in enumerate(
            [(nodes, nodev), (x.at[:, :, :, columns(me)], recv.at[:, me]), (inv, invv), (fwd, fwdv)]
        )
    ]
    for c in loads:
        c.start()
    pl.semaphore_wait(bar, 15 + has_prev.astype(jnp.int32) + has_next.astype(jnp.int32))

    first = []
    for h in range(2):
        part = pl.ds(6 * h, 6)
        for i, t in enumerate(peers):
            c = pltpu.make_async_remote_copy(
                x.at[part, :, :, columns(t)], recv.at[part, me], s1.at[h, i], r1.at[h, i],
                device_id={"mode": t}, device_id_type=MESH,
            )
            c.start()
            first.append(c)

    loads[0].wait()

    def choose(i, carry):
        at = lax.broadcasted_iota(jnp.int32, (TILE, HALO), 0) + i * TILE
        for side in range(2):
            apart = jnp.abs(at - nodev[side : side + 1, :])
            hit = jnp.maximum(1 - apart, 0).astype(jnp.float32)
            gath[columns(i), side * HALO : (side + 1) * HALO] = hit.astype(jnp.bfloat16)
        return carry

    lax.fori_loop(0, NODES // TILE, choose, 0)
    for c in loads[1:]:
        c.wait()
    fields = recv.reshape(12, 2 * M, TILE)

    def inverse(h):
        for c in first[15 * h : 15 * h + 15]:
            c.wait_recv()
        for c in range(6 * h, 6 * h + 6, 2):
            both = dot(invv[...], jnp.concatenate([fields[c], fields[c + 1]], axis=1))
            phys[c] = both[:, :TILE]
            phys[c + 1] = both[:, TILE:]

    def forward(c, n):
        for k in range(c, c + n, 2):
            if k + 1 < c + n:
                both = dot(fwdv[...], jnp.concatenate([prod[k], prod[k + 1]], axis=1)).astype(jnp.bfloat16)
                send[k] = both[:, :TILE]
                send[k + 1] = both[:, TILE:]
            else:
                send[k] = dot(fwdv[...], prod[k]).astype(jnp.bfloat16)

    def give(c, n, into, h):
        out = []
        for i, t in enumerate(peers):
            copy = pltpu.make_async_remote_copy(
                send.at[pl.ds(c, n), rows(t), :], into.at[:, :, columns(me)], s2.at[h, i], r2.at[h, i],
                device_id={"mode": t}, device_id_type=MESH,
            )
            copy.start()
            out.append(copy)
        into[:, :, columns(me)] = send[c : c + n, rows(me), :]
        return out

    def cross(a, b):
        return [a[1] * b[2] - a[2] * b[1], a[2] * b[0] - a[0] * b[2], a[0] * b[1] - a[1] * b[0]]

    step = 32
    inverse(0)

    def early(i, carry):
        at = pl.ds(pl.multiple_of(i * step, step), step)
        v = [phys[c, at, :] for c in range(3)]
        b = [phys[c, at, :] for c in range(3, 6)]
        f = cross(v, b)
        for c in range(3):
            prod[c, at, :] = f[c].astype(jnp.bfloat16)
        prod[3, at, :] = (0.5 * (v[0] * v[0] + v[1] * v[1] + v[2] * v[2])).astype(jnp.bfloat16)
        return carry

    lax.fori_loop(0, THETA // step, early, 0)
    forward(0, 4)
    second = give(0, 4, ext, 0)
    inverse(1)

    def late(i, carry):
        at = pl.ds(pl.multiple_of(i * step, step), step)
        v, b, j, w = ([phys[c, at, :] for c in range(k, k + 3)] for k in (0, 3, 6, 9))
        f, g = cross(j, b), cross(v, w)
        for c in range(3):
            prod[4 + c, at, :] = (f[c] + g[c]).astype(jnp.bfloat16)
        return carry

    lax.fori_loop(0, THETA // step, late, 0)
    forward(4, 3)
    third = give(4, 3, lor, 1)

    for c in second:
        c.wait_recv()
    own = pltpu.make_async_copy(ext.at[:, :, pl.ds(0, NODES)], out_ext.at[:, :, pl.ds(0, NODES)], osem.at[0])
    own.start()
    halo[...] = (
        dot(ext[:, :, :NODES].reshape(4 * ROWS, NODES), gath[...])
        .astype(jnp.bfloat16)
        .reshape(4, ROWS, 2 * HALO)
    )
    to_prev = pltpu.make_async_remote_copy(
        halo.at[:, :, pl.ds(0, HALO)], ext.at[:, :, pl.ds(NODES + HALO, HALO)], sh.at[0], rh.at[0],
        device_id={"mer": dom - 1}, device_id_type=MESH,
    )
    to_next = pltpu.make_async_remote_copy(
        halo.at[:, :, pl.ds(HALO, HALO)], ext.at[:, :, pl.ds(NODES, HALO)], sh.at[1], rh.at[1],
        device_id={"mer": dom + 1}, device_id_type=MESH,
    )
    pl.when(has_prev)(to_prev.start)
    pl.when(has_next)(to_next.start)

    @pl.when(has_next)
    def _():
        to_prev.wait_recv()

    @pl.when(jnp.logical_not(has_next))
    def _():
        ext[:, :, NODES + HALO :] = jnp.zeros((4, ROWS, HALO), jnp.bfloat16)

    @pl.when(has_prev)
    def _():
        to_next.wait_recv()

    @pl.when(jnp.logical_not(has_prev))
    def _():
        ext[:, :, NODES : NODES + HALO] = jnp.zeros((4, ROWS, HALO), jnp.bfloat16)

    edge = pltpu.make_async_copy(
        ext.at[:, :, pl.ds(NODES, 2 * HALO)], out_ext.at[:, :, pl.ds(NODES, 2 * HALO)], osem.at[1]
    )
    edge.start()
    for c in third:
        c.wait_recv()
    force = pltpu.make_async_copy(lor, out_lor, osem.at[2])
    force.start()
    for c in first + second + third:
        c.wait_send()
    pl.when(has_prev)(to_prev.wait_send)
    pl.when(has_next)(to_next.wait_send)
    own.wait()
    edge.wait()
    force.wait()


def combine(cols, ext_in, lor, radius, rad, axi, ind, mom, ext):
    me = lax.axis_index("mode")
    wide = 2 * TILE
    turn_r = lax.broadcasted_iota(jnp.int32, (TILE, TILE), 0)
    turn_c = lax.broadcasted_iota(jnp.int32, (TILE, TILE), 1)
    turn = jnp.where((turn_r + BLK) % TILE == turn_c, 1.0, 0.0).astype(jnp.bfloat16)

    def swap(i, carry):
        at = pl.ds(pl.multiple_of(i * TILE, TILE), TILE)
        value = ext_in[:, :, at].reshape(4 * ROWS, TILE)
        ext[0, :, at] = value
        ext[1, :, at] = dot(value, turn).astype(jnp.bfloat16)
        return carry

    lax.fori_loop(0, EXT // TILE, swap, 0, unroll=4)
    low = lax.broadcasted_iota(jnp.int32, (4 * ROWS, TILE), 1) < BLK
    mode = (me * HALF + lax.broadcasted_iota(jnp.int32, (HALF, TILE), 0)).astype(jnp.float32)

    def derive(j, carry):
        at = pl.ds(pl.multiple_of(j * TILE, TILE), TILE)
        lhs = []
        for half in range(2):
            tiles = []
            for k in range(NNZB):
                block = cols[k, 2 * j + half]
                where = pl.ds(pl.multiple_of((block // 2) * TILE, TILE), TILE)
                tiles.append(ext[(block + k) % 2, :, where])
            tiles.append(jnp.zeros_like(tiles[0]))
            lhs.append(
                jnp.concatenate([jnp.where(low, tiles[k], tiles[k + 1]) for k in (0, 2, 4)], axis=1)
            )
        rhs = jnp.concatenate([rad[:, at], axi[:, at]], axis=1)
        rhs = jnp.concatenate([rhs, jnp.zeros((DEPTH - NNZB * BLK, wide), jnp.bfloat16)], axis=0)
        both = dot(jnp.concatenate(lhs, axis=0), rhs)
        n = 4 * ROWS
        along_r = jnp.where(low, both[:n, :TILE], both[n:, :TILE])
        along_z = jnp.where(low, both[:n, TILE:], both[n:, TILE:])
        local = ext[0, :, at].astype(jnp.float32)
        over = 1.0 / radius[pl.ds(j, 1), :]

        def part(a, c):
            return a[c * ROWS : (c + 1) * ROWS]

        def rotated(c):
            v = part(local, c)
            return jnp.concatenate([-mode * v[HALF:], mode * v[:HALF]], axis=0) * over

        def put(out, c, value):
            for p in range(2):
                out[pl.ds(c * 2 * M + 2 * j + p, HALF, 32), :] = value[p * HALF : (p + 1) * HALF]

        put(ind, 0, rotated(2) - part(along_z, 1))
        put(ind, 1, part(along_z, 0) - part(along_r, 2))
        put(ind, 2, part(along_r, 1) + part(local, 1) * over - rotated(0))
        put(mom, 0, lor[0, :, at].astype(jnp.float32) - part(along_r, 3))
        put(mom, 1, lor[1, :, at].astype(jnp.float32) - rotated(3))
        put(mom, 2, lor[2, :, at].astype(jnp.float32) - part(along_z, 3))
        return carry

    lax.fori_loop(0, NODES // TILE, derive, 0, unroll=2)


def body(mode_fields, radius, radial_blocks, axial_blocks, block_columns, interface_nodes):
    bf, f32 = jnp.bfloat16, jnp.float32
    inv, fwd = tables()
    dma = pltpu.SemaphoreType.DMA
    anywhere, vmem = pl.BlockSpec(memory_space=pl.ANY), pl.BlockSpec(memory_space=pltpu.VMEM)
    ext, lor = pl.pallas_call(
        exchange,
        out_shape=[jax.ShapeDtypeStruct((4, ROWS, EXT), bf), jax.ShapeDtypeStruct((3, ROWS, NODES), bf)],
        in_specs=[anywhere] * 4,
        out_specs=[anywhere] * 2,
        scratch_shapes=[
            pltpu.VMEM((12, 16, HALF, 2, TILE), bf),
            pltpu.VMEM((12, THETA, TILE), f32),
            pltpu.VMEM((7, THETA, TILE), bf),
            pltpu.VMEM((7, 2 * M, TILE), bf),
            pltpu.VMEM((4, ROWS, EXT), bf),
            pltpu.VMEM((3, ROWS, NODES), bf),
            pltpu.VMEM((NODES, 2 * HALO), bf),
            pltpu.VMEM((4, ROWS, 2 * HALO), bf),
            pltpu.VMEM((THETA, 2 * M), bf),
            pltpu.VMEM((2 * M, THETA), bf),
            pltpu.VMEM((2, HALO), jnp.int32),
            dma((4,)), dma((3,)),
            dma((2, 15)), dma((2, 15)), dma((2, 15)), dma((2, 15)), dma((2,)), dma((2,)),
        ],
        compiler_params=pltpu.CompilerParams(
            collective_id=0, has_side_effects=True, vmem_limit_bytes=40 * 1024 * 1024
        ),
    )(mode_fields, inv, fwd, interface_nodes)
    ind, mom = pl.pallas_call(
        combine,
        out_shape=[jax.ShapeDtypeStruct((3 * 2 * M, TILE), f32)] * 2,
        in_specs=[pl.BlockSpec(memory_space=pltpu.SMEM)] + [vmem] * 5,
        out_specs=[vmem] * 2,
        scratch_shapes=[pltpu.VMEM((2, 4 * ROWS, EXT), bf)],
        compiler_params=pltpu.CompilerParams(vmem_limit_bytes=24 * 1024 * 1024),
    )(
        block_columns.T, ext, lor, radius.reshape(NODES // TILE, TILE),
        radial_blocks.reshape(NNZB * BLK, NODES), axial_blocks.reshape(NNZB * BLK, NODES),
    )

    def whole(a):
        a = a.reshape(3, HALF, NODES // TILE, 2, TILE)
        return a.transpose(0, 1, 3, 2, 4).reshape(3, HALF, 2, NODES)

    return whole(ind), whole(mom)


def solution(mesh):
    placed = (
        P(None, "mode", None, "mer"),
        P("mer"),
        P(None, None, "mer"),
        P(None, None, "mer"),
        P("mer", None),
        P("mer", None),
    )
    return jax.shard_map(
        body,
        mesh=mesh,
        in_specs=placed,
        out_specs=(P(None, "mode", None, "mer"), P(None, "mode", None, "mer")),
        check_vma=False,
    )
```

time: 143 us -> 90.5 us (0.63)
  the two profiles are of different devices: /device:TPU:26 before, /device:TPU:72 now
where the time goes in v1:
time: 90.5 us; the launch traced here: 90.2 us
  Pallas kernels  81.9 us (90%)
  local copies, waits for them, and re-layouts  7.62 us (8%)
    pallas_call x1, Pallas kernels, body(): pl.pallas_call(exchange, out_shape=[jax.ShapeDtypeStruct((4, ROWS, EXT),...  76.4 us
    unnamed x16, local copies, waits for them, and re-layouts  7.62 us
    pallas_call x1, Pallas kernels, body(): pl.pallas_call(combine, out_shape=[jax.ShapeDtypeStruct((3 * 2 * M, TILE)...  5.51 us

profile of v1, /device:TPU:72, one launch (start us, length us, event | category | flops | bytes accessed | tf_op | source)
XLA Modules:
  0.0 90.2 jit_solution(15344728650564605892)
XLA Ops:
  0.6 0.0 copy-start.2
  0.6 1.1 %copy-done.2 = bf16[12,8,2,2048]{3,2,1,0:T(2,128)(2,1)S(1)} copy-done((bf16[12,8,2,2048]{3,2,1,0:T(2,128)(2,1)S(1)}, bf16[12,8,2,2048]{3,2,1,0:T(2,128)(2,1)}, u32[]{:S(2)}) %copy-start.2) | copy-done | bytes 786456
  1.8 0.0 copy-start.3
  1.8 0.9 %copy-done.3 = bf16[256,256]{1,0:T(8,128)(2,1)S(1)} copy-done((bf16[256,256]{1,0:T(8,128)(2,1)S(1)}, bf16[256,256]{1,0:T(8,128)(2,1)}, u32[]{:S(2)}) %copy-start.3) | copy-done | bytes 131096
  2.7 0.0 copy-start.4
  2.7 0.9 %copy-done.4 = bf16[256,256]{1,0:T(8,128)(2,1)S(1)} copy-done((bf16[256,256]{1,0:T(8,128)(2,1)S(1)}, bf16[256,256]{1,0:T(8,128)(2,1)}, u32[]{:S(2)}) %copy-start.4) | copy-done | bytes 131096
  3.6 0.0 copy-start.7
  3.6 0.7 copy-done.7
  4.3 76.4 %shard_map.95 = (bf16[4,16,2560]{2,1,0:T(8,128)(2,1)S(1)}, bf16[3,16,2048]{2,1,0:T(8,128)(2,1)S(1)}) custom-call(bf16[12,8,2,2048]{3,2,1,0:T(2,128)(2,1)S(1)} %copy-done.2, bf16[256,256]{1,0:T(8,128)(2,1)S(1)} %copy-done.4, bf16[256,256]{1,0:T(8,128)(2,1)S(1)} %copy-done.3, s32[2,256]{1,0:T(2,128)S(1)} %copy-done.7), custom_call_target="tpu_custom_call" | custom-call | tf_op jit(solution)/shard_map/pallas_call | solution.py:291
  80.6 0.0 copy-start
  80.6 1.3 %copy-done = bf16[5,64,2048]{2,1,0:T(8,128)(2,1)S(1)} copy-done((bf16[5,64,2048]{2,1,0:T(8,128)(2,1)S(1)}, bf16[5,64,2048]{2,1,0:T(8,128)(2,1)}, u32[]{:S(2)}) %copy-start) | copy-done | bytes 1310744
  81.9 0.0 copy-start.1
  81.9 1.3 %copy-done.1 = bf16[5,64,2048]{2,1,0:T(8,128)(2,1)S(1)} copy-done((bf16[5,64,2048]{2,1,0:T(8,128)(2,1)S(1)}, bf16[5,64,2048]{2,1,0:T(8,128)(2,1)}, u32[]{:S(2)}) %copy-start.1) | copy-done | bytes 1310744
  83.3 0.0 copy-start.5
  83.3 0.7 copy-done.5
  84.0 0.0 copy-start.6
  84.0 0.7 copy-done.6
  84.6 5.5 %shard_map.96 = (f32[768,128]{1,0:T(8,128)}, f32[768,128]{1,0:T(8,128)}) custom-call(s32[5,32]{1,0:T(8,128)S(1)} %bitcast.17, bf16[4,16,2560]{2,1,0:T(8,128)(2,1)S(1)} %get-tuple-element.6.ext_in, bf16[3,16,2048]{2,1,0:T(8,128)(2,1)S(1)} %get-tuple-element.7.lor, f32[16,128]{1,0:T(8,128)S(1)} %bitcast.16, bf16[320,2048]{1,0:T(8,128)(2,1)S(1)} %bitcast.14, ...), custom_call_target="tpu_custom_call" | custom-call | tf_op jit(solution)/shard_map/pallas_call | solution.py:315
Async XLA Ops:
  0.6 1.1 %copy-start.2 = (bf16[12,8,2,2048]{3,2,1,0:T(2,128)(2,1)S(1)}, bf16[12,8,2,2048]{3,2,1,0:T(2,128)(2,1)}, u32[]{:S(2)}) copy-start(bf16[12,8,2,2048]{3,2,1,0:T(2,128)(2,1)} %x.1) | copy-start | bytes 2359300
  1.8 0.9 %copy-start.3 = (bf16[256,256]{1,0:T(8,128)(2,1)S(1)}, bf16[256,256]{1,0:T(8,128)(2,1)}, u32[]{:S(2)}) copy-start(bf16[256,256]{1,0:T(8,128)(2,1)} %constant.5.clone.fwd) | copy-start | bytes 393220
  2.7 0.9 %copy-start.4 = (bf16[256,256]{1,0:T(8,128)(2,1)S(1)}, bf16[256,256]{1,0:T(8,128)(2,1)}, u32[]{:S(2)}) copy-start(bf16[256,256]{1,0:T(8,128)(2,1)} %constant.4.clone.inv) | copy-start | bytes 393220
  3.6 0.7 copy-start.7
  80.6 1.3 %copy-start = (bf16[5,64,2048]{2,1,0:T(8,128)(2,1)S(1)}, bf16[5,64,2048]{2,1,0:T(8,128)(2,1)}, u32[]{:S(2)}) copy-start(bf16[5,64,2048]{2,1,0:T(8,128)(2,1)} %param.10) | copy-start | bytes 3932164
  81.9 1.3 %copy-start.1 = (bf16[5,64,2048]{2,1,0:T(8,128)(2,1)S(1)}, bf16[5,64,2048]{2,1,0:T(8,128)(2,1)}, u32[]{:S(2)}) copy-start(bf16[5,64,2048]{2,1,0:T(8,128)(2,1)} %param.11) | copy-start | bytes 3932164
  83.3 0.7 copy-start.5
  84.0 0.7 copy-start.6

commit v2 on v1

v2 whole, which is shorter than its diff:
```python
import functools
import math

import jax
import jax.numpy as jnp
import numpy as np
from jax import lax
from jax.experimental import pallas as pl
from jax.experimental.pallas import tpu as pltpu
from jax.sharding import PartitionSpec as P

M = 128
THETA = 256
BLK = 64
NNZB = 5
MESH = pl.DeviceIdType.MESH
PEERS = [(dx, dz) for dz in (2, 1, 3, 0) for dx in (0, 1, 2, 3) if (dx, dz) != (0, 0)]
ROWS = 16
HALF = ROWS // 2
NODES = 2048
HALO = 256
EXT = NODES + 2 * HALO
TILE = 128
DEPTH = 384


def tables():
    modes = np.arange(M, dtype=np.int32)
    angles = np.arange(THETA, dtype=np.int32)
    phase = (angles[:, None] * modes[None, :]) % THETA
    angle = phase.astype(np.float32) * np.float32(2.0 * math.pi / THETA)
    weight = np.where(modes == 0, 1.0, 2.0).astype(np.float32)
    cosines, sines = np.cos(angle), np.sin(angle)
    inverse = np.stack([weight * cosines, -weight * sines], axis=-1).reshape(THETA, 2 * M)
    forward = np.stack([cosines.T, -sines.T], axis=0) / np.float32(THETA)
    forward = forward.reshape(2, 16, M // 16, THETA).transpose(1, 0, 2, 3).reshape(2 * M, THETA)
    return jnp.asarray(inverse.astype(jnp.bfloat16)), jnp.asarray(forward.astype(jnp.bfloat16))


def dot(a, b):
    return jnp.dot(a, b, preferred_element_type=jnp.float32)


def kernel(
    x, inv, fwd, nodes, radius, rad, axi, cols, ind, mom,
    recv, phys, prod, send, ext, lor, gath, halo, blocks, rest, indv, momv, rv, zv, invv, fwdv, nodev, radv, colv,
    lsem, osem, s1, r1, s2, r2, sh, rh,
):
    me, dom = lax.axis_index("mode"), lax.axis_index("mer")
    doms = lax.axis_size("mer")
    mx, mz = me // 4, me % 4
    peers = [lax.rem(mx + dx, 4) * 4 + lax.rem(mz + dz, 4) for dx, dz in PEERS]
    has_prev, has_next = dom > 0, dom < doms - 1

    bar = pltpu.get_barrier_semaphore()
    for t in peers:
        pl.semaphore_signal(bar, inc=1, device_id={"mode": t}, device_id_type=MESH)

    @pl.when(has_prev)
    def _():
        pl.semaphore_signal(bar, inc=1, device_id={"mer": dom - 1}, device_id_type=MESH)

    @pl.when(has_next)
    def _():
        pl.semaphore_signal(bar, inc=1, device_id={"mer": dom + 1}, device_id_type=MESH)

    def columns(t):
        return pl.ds(pl.multiple_of(t * TILE, TILE), TILE)

    def rows(t):
        return pl.ds(pl.multiple_of(t * ROWS, ROWS), ROWS)

    stored = pl.ds(0, NNZB * BLK)
    loads = [
        pltpu.make_async_copy(a, b, lsem.at[i])
        for i, (a, b) in enumerate(
            [
                (nodes, nodev),
                (x.at[:, :, :, columns(me)], recv.at[:, me]),
                (inv, invv),
                (fwd, fwdv),
                (cols, colv),
                (radius, radv),
                (rad, rv.at[stored, :]),
                (axi, zv.at[stored, :]),
            ]
        )
    ]
    for c in loads:
        c.start()
    pl.semaphore_wait(bar, 15 + has_prev.astype(jnp.int32) + has_next.astype(jnp.int32))

    first = []
    for h in range(2):
        part = pl.ds(6 * h, 6)
        for i, t in enumerate(peers):
            c = pltpu.make_async_remote_copy(
                x.at[part, :, :, columns(t)], recv.at[part, me], s1.at[h, i], r1.at[h, i],
                device_id={"mode": t}, device_id_type=MESH,
            )
            c.start()
            first.append(c)

    loads[0].wait()

    def choose(i, carry):
        at = lax.broadcasted_iota(jnp.int32, (TILE, HALO), 0) + i * TILE
        for side in range(2):
            apart = jnp.abs(at - nodev[side : side + 1, :])
            hit = jnp.maximum(1 - apart, 0).astype(jnp.float32)
            gath[columns(i), side * HALO : (side + 1) * HALO] = hit.astype(jnp.bfloat16)
        return carry

    lax.fori_loop(0, NODES // TILE, choose, 0)
    for v in (rv, zv):
        v[NNZB * BLK :, :] = jnp.zeros((DEPTH - NNZB * BLK, NODES), jnp.bfloat16)
    for c in loads[1:]:
        c.wait()
    fields = recv.reshape(12, 2 * M, TILE)

    def inverse(h):
        for c in first[15 * h : 15 * h + 15]:
            c.wait_recv()
        for c in range(6 * h, 6 * h + 6, 2):
            both = dot(invv[...], jnp.concatenate([fields[c], fields[c + 1]], axis=1))
            phys[c] = both[:, :TILE]
            phys[c + 1] = both[:, TILE:]

    def forward(c, n):
        for k in range(c, c + n, 2):
            if k + 1 < c + n:
                both = dot(fwdv[...], jnp.concatenate([prod[k], prod[k + 1]], axis=1)).astype(jnp.bfloat16)
                send[k] = both[:, :TILE]
                send[k + 1] = both[:, TILE:]
            else:
                send[k] = dot(fwdv[...], prod[k]).astype(jnp.bfloat16)

    def give(c, n, into, h):
        out = []
        for i, t in enumerate(peers):
            copy = pltpu.make_async_remote_copy(
                send.at[pl.ds(c, n), rows(t), :], into.at[me], s2.at[h, i], r2.at[h, i],
                device_id={"mode": t}, device_id_type=MESH,
            )
            copy.start()
            out.append(copy)
        into[me] = send[c : c + n, rows(me), :]
        return out

    def cross(a, b):
        return [a[1] * b[2] - a[2] * b[1], a[2] * b[0] - a[0] * b[2], a[0] * b[1] - a[1] * b[0]]

    step = 32
    inverse(0)

    def early(i, carry):
        at = pl.ds(pl.multiple_of(i * step, step), step)
        v = [phys[c, at, :] for c in range(3)]
        b = [phys[c, at, :] for c in range(3, 6)]
        f = cross(v, b)
        for c in range(3):
            prod[c, at, :] = f[c].astype(jnp.bfloat16)
        prod[3, at, :] = (0.5 * (v[0] * v[0] + v[1] * v[1] + v[2] * v[2])).astype(jnp.bfloat16)
        return carry

    lax.fori_loop(0, THETA // step, early, 0)
    forward(0, 4)
    second = give(0, 4, ext, 0)
    inverse(1)

    def late(i, carry):
        at = pl.ds(pl.multiple_of(i * step, step), step)
        v, b, j, w = ([phys[c, at, :] for c in range(k, k + 3)] for k in (0, 3, 6, 9))
        f, g = cross(j, b), cross(v, w)
        for c in range(3):
            prod[4 + c, at, :] = (f[c] + g[c]).astype(jnp.bfloat16)
        return carry

    lax.fori_loop(0, THETA // step, late, 0)
    forward(4, 3)
    third = give(4, 3, lor, 1)

    tiles = NODES // TILE
    side = HALO // TILE
    for c in second:
        c.wait_recv()
    own = jnp.concatenate([ext[i].reshape(4 * ROWS, TILE) for i in range(tiles)], axis=1)
    edge = dot(own, gath[...]).astype(jnp.bfloat16)
    for i in range(2 * side):
        halo[i] = edge[:, i * TILE : (i + 1) * TILE].reshape(4, ROWS, TILE)
    to_prev = pltpu.make_async_remote_copy(
        halo.at[pl.ds(0, side)], ext.at[pl.ds(tiles + side, side)], sh.at[0], rh.at[0],
        device_id={"mer": dom - 1}, device_id_type=MESH,
    )
    to_next = pltpu.make_async_remote_copy(
        halo.at[pl.ds(side, side)], ext.at[pl.ds(tiles, side)], sh.at[1], rh.at[1],
        device_id={"mer": dom + 1}, device_id_type=MESH,
    )
    pl.when(has_prev)(to_prev.start)
    pl.when(has_next)(to_next.start)

    turn_r = lax.broadcasted_iota(jnp.int32, (TILE, TILE), 0)
    turn_c = lax.broadcasted_iota(jnp.int32, (TILE, TILE), 1)
    turn = jnp.where((turn_r + BLK) % TILE == turn_c, 1.0, 0.0).astype(jnp.bfloat16)

    def spread(i, carry):
        value = ext[i].reshape(4 * ROWS, TILE)
        turned = dot(value, turn).astype(jnp.bfloat16)
        blocks[0, 2 * i] = value
        blocks[1, 2 * i] = turned
        blocks[0, 2 * i + 1] = turned
        blocks[1, 2 * i + 1] = value
        return carry

    lax.fori_loop(0, tiles, spread, 0)

    @pl.when(has_next)
    def _():
        to_prev.wait_recv()

    @pl.when(jnp.logical_not(has_next))
    def _():
        ext[tiles + side :] = jnp.zeros((side, 4, ROWS, TILE), jnp.bfloat16)

    @pl.when(has_prev)
    def _():
        to_next.wait_recv()

    @pl.when(jnp.logical_not(has_prev))
    def _():
        ext[tiles : tiles + side] = jnp.zeros((side, 4, ROWS, TILE), jnp.bfloat16)

    lax.fori_loop(tiles, tiles + 2 * side, spread, 0)

    low = lax.broadcasted_iota(jnp.int32, (4 * ROWS, TILE), 1) < BLK
    mode = (me * HALF + lax.broadcasted_iota(jnp.int32, (HALF, TILE), 0)).astype(jnp.float32)

    def put(out, j, c, value):
        for p in range(2):
            out[pl.ds(c * 2 * M + 2 * j + p, HALF, 32), :] = value[p * HALF : (p + 1) * HALF]

    def derive(j, carry):
        lhs = []
        for half in range(2):
            picked = [blocks[k % 2, colv[k, 2 * j + half]] for k in range(NNZB)]
            picked.append(jnp.zeros_like(picked[0]))
            lhs.append(
                jnp.concatenate([jnp.where(low, picked[k], picked[k + 1]) for k in (0, 2, 4)], axis=1)
            )
        rhs = jnp.concatenate([rv[:, columns(j)], zv[:, columns(j)]], axis=1)
        both = dot(jnp.concatenate(lhs, axis=0), rhs)
        n = 4 * ROWS
        along_r = jnp.where(low, both[:n, :TILE], both[n:, :TILE])
        along_z = jnp.where(low, both[:n, TILE:], both[n:, TILE:])
        local = [ext[j, c].astype(jnp.float32) for c in range(4)]
        over = 1.0 / radv[pl.ds(j, 1), :]

        def part(a, c):
            return a[c * ROWS : (c + 1) * ROWS]

        def rotated(v):
            return jnp.concatenate([-mode * v[HALF:], mode * v[:HALF]], axis=0) * over

        put(indv, j, 0, rotated(local[2]) - part(along_z, 1))
        put(indv, j, 1, part(along_z, 0) - part(along_r, 2))
        put(indv, j, 2, part(along_r, 1) + local[1] * over - rotated(local[0]))
        rest[j, 0] = part(along_r, 3)
        rest[j, 1] = rotated(local[3])
        rest[j, 2] = part(along_z, 3)
        return carry

    lax.fori_loop(0, tiles, derive, 0)
    out0 = pltpu.make_async_copy(indv, ind, osem.at[0])
    out0.start()

    for c in third:
        c.wait_recv()

    def finish(j, carry):
        for c in range(3):
            put(momv, j, c, lor[j, c].astype(jnp.float32) - rest[j, c])
        return carry

    lax.fori_loop(0, tiles, finish, 0)
    out1 = pltpu.make_async_copy(momv, mom, osem.at[1])
    out1.start()
    for c in first + second + third:
        c.wait_send()
    pl.when(has_prev)(to_prev.wait_send)
    pl.when(has_next)(to_next.wait_send)
    out0.wait()
    out1.wait()


def body(mode_fields, radius, radial_blocks, axial_blocks, block_columns, interface_nodes):
    bf, f32 = jnp.bfloat16, jnp.float32
    inv, fwd = tables()
    dma = pltpu.SemaphoreType.DMA
    anywhere = pl.BlockSpec(memory_space=pl.ANY)
    tiles = NODES // TILE
    ind, mom = pl.pallas_call(
        kernel,
        out_shape=[jax.ShapeDtypeStruct((3 * 2 * M, TILE), f32)] * 2,
        in_specs=[anywhere] * 8,
        out_specs=[anywhere] * 2,
        scratch_shapes=[
            pltpu.VMEM((12, 16, HALF, 2, TILE), bf),
            pltpu.VMEM((12, THETA, TILE), f32),
            pltpu.VMEM((7, THETA, TILE), bf),
            pltpu.VMEM((7, 2 * M, TILE), bf),
            pltpu.VMEM((EXT // TILE, 4, ROWS, TILE), bf),
            pltpu.VMEM((tiles, 3, ROWS, TILE), bf),
            pltpu.VMEM((NODES, 2 * HALO), bf),
            pltpu.VMEM((2 * HALO // TILE, 4, ROWS, TILE), bf),
            pltpu.VMEM((2, EXT // BLK, 4 * ROWS, TILE), bf),
            pltpu.VMEM((tiles, 3, ROWS, TILE), f32),
            pltpu.VMEM((3 * 2 * M, TILE), f32),
            pltpu.VMEM((3 * 2 * M, TILE), f32),
            pltpu.VMEM((DEPTH, NODES), bf),
            pltpu.VMEM((DEPTH, NODES), bf),
            pltpu.VMEM((THETA, 2 * M), bf),
            pltpu.VMEM((2 * M, THETA), bf),
            pltpu.VMEM((2, HALO), jnp.int32),
            pltpu.VMEM((tiles, TILE), f32),
            pltpu.SMEM((NNZB, NODES // BLK), jnp.int32),
            dma((8,)), dma((2,)),
            dma((2, 15)), dma((2, 15)), dma((2, 15)), dma((2, 15)), dma((2,)), dma((2,)),
        ],
        compiler_params=pltpu.CompilerParams(
            collective_id=0, has_side_effects=True, vmem_limit_bytes=56 * 1024 * 1024
        ),
    )(
        mode_fields, inv, fwd, interface_nodes, radius.reshape(tiles, TILE),
        radial_blocks.reshape(NNZB * BLK, NODES), axial_blocks.reshape(NNZB * BLK, NODES), block_columns.T,
    )

    def whole(a):
        a = a.reshape(3, HALF, tiles, 2, TILE)
        return a.transpose(0, 1, 3, 2, 4).reshape(3, HALF, 2, NODES)

    return whole(ind), whole(mom)


def solution(mesh):
    placed = (
        P(None, "mode", None, "mer"),
        P("mer"),
        P(None, None, "mer"),
        P(None, None, "mer"),
        P("mer", None),
        P("mer", None),
    )
    return jax.shard_map(
        body,
        mesh=mesh,
        in_specs=placed,
        out_specs=(P(None, "mode", None, "mer"), P(None, "mode", None, "mer")),
        check_vma=False,
    )
```

time: 90.5 us -> 84.9 us (0.938)
  the two profiles are of different devices: /device:TPU:72 before, /device:TPU:8 now
where the time goes in v2:
time: 84.9 us; the launch traced here: 84.7 us
  Pallas kernels  80.5 us (95%)
  local copies, waits for them, and re-layouts  3.53 us (4%)
    pallas_call x1, Pallas kernels, body(): pl.pallas_call(kernel, out_shape=[jax.ShapeDtypeStruct((3 * 2 * M, TILE),...  80.5 us
    unnamed x2, local copies, waits for them, and re-layouts  3.53 us

profile of v2, /device:TPU:8, one launch (start us, length us, event | category | flops | bytes accessed | tf_op | source)
XLA Modules:
  0.0 84.7 jit_solution(5809681678113280317)
XLA Ops:
  0.6 80.5 %shard_map.95 = (f32[768,128]{1,0:T(8,128)}, f32[768,128]{1,0:T(8,128)}) custom-call(bf16[12,8,2,2048]{3,2,1,0:T(2,128)(2,1)} %x.1, bf16[256,256]{1,0:T(8,128)(2,1)} %constant.4.clone.inv, bf16[256,256]{1,0:T(8,128)(2,1)} %constant.5.clone.fwd, s32[2,256]{1,0:T(2,128)} %nodes.1, f32[16,128]{1,0:T(8,128)} %bitcast.18, bf16[320,2048]{1,0:T(8,128)(2,1)} %bitcast.14, ...), custom_call_target="tpu_custom_call" | custom-call | tf_op jit(solution)/shard_map/pallas_call | solution.py:301
  81.2 1.8 %copy.14 = f32[3,8,2,2048]{3,2,1,0:T(2,128)} copy(f32[3,8,2,2048]{3,2,1,0:T(2,128)} %bitcast.17) | data formatting | bytes 786432
  82.9 1.8 %copy.15 = f32[3,8,2,2048]{3,2,1,0:T(2,128)} copy(f32[3,8,2,2048]{3,2,1,0:T(2,128)} %bitcast.16) | data formatting | bytes 786432

commit v3 on v2

--- a/solution.py
+++ b/solution.py
@@ -43,8 +43,8 @@
 
 def kernel(
     x, inv, fwd, nodes, radius, rad, axi, cols, ind, mom,
-    recv, phys, prod, send, ext, lor, gath, halo, blocks, rest, indv, momv, rv, zv, invv, fwdv, nodev, radv, colv,
-    lsem, osem, s1, r1, s2, r2, sh, rh,
+    recv, phys, prod, send, ext, lor, gath, halo, blocks, rest, rv, zv, invv, fwdv, nodev, radv, colv,
+    lsem, s1, r1, s2, r2, sh, rh,
 ):
     me, dom = lax.axis_index("mode"), lax.axis_index("mer")
     doms = lax.axis_size("mer")
@@ -212,7 +212,7 @@
         blocks[1, 2 * i + 1] = value
         return carry
 
-    lax.fori_loop(0, tiles, spread, 0)
+    lax.fori_loop(0, tiles, spread, 0, unroll=4)
 
     @pl.when(has_next)
     def _():
@@ -230,7 +230,7 @@
     def _():
         ext[tiles : tiles + side] = jnp.zeros((side, 4, ROWS, TILE), jnp.bfloat16)
 
-    lax.fori_loop(tiles, tiles + 2 * side, spread, 0)
+    lax.fori_loop(tiles, tiles + 2 * side, spread, 0, unroll=True)
 
     low = lax.broadcasted_iota(jnp.int32, (4 * ROWS, TILE), 1) < BLK
     mode = (me * HALF + lax.broadcasted_iota(jnp.int32, (HALF, TILE), 0)).astype(jnp.float32)
@@ -261,35 +261,29 @@
         def rotated(v):
             return jnp.concatenate([-mode * v[HALF:], mode * v[:HALF]], axis=0) * over
 
-        put(indv, j, 0, rotated(local[2]) - part(along_z, 1))
-        put(indv, j, 1, part(along_z, 0) - part(along_r, 2))
-        put(indv, j, 2, part(along_r, 1) + local[1] * over - rotated(local[0]))
+        put(ind, j, 0, rotated(local[2]) - part(along_z, 1))
+        put(ind, j, 1, part(along_z, 0) - part(along_r, 2))
+        put(ind, j, 2, part(along_r, 1) + local[1] * over - rotated(local[0]))
         rest[j, 0] = part(along_r, 3)
         rest[j, 1] = rotated(local[3])
         rest[j, 2] = part(along_z, 3)
         return carry
 
-    lax.fori_loop(0, tiles, derive, 0)
-    out0 = pltpu.make_async_copy(indv, ind, osem.at[0])
-    out0.start()
+    lax.fori_loop(0, tiles, derive, 0, unroll=4)
 
     for c in third:
         c.wait_recv()
 
     def finish(j, carry):
         for c in range(3):
-            put(momv, j, c, lor[j, c].astype(jnp.float32) - rest[j, c])
-        return carry
-
-    lax.fori_loop(0, tiles, finish, 0)
-    out1 = pltpu.make_async_copy(momv, mom, osem.at[1])
-    out1.start()
+            put(mom, j, c, lor[j, c].astype(jnp.float32) - rest[j, c])
+        return carry
+
+    lax.fori_loop(0, tiles, finish, 0, unroll=4)
     for c in first + second + third:
         c.wait_send()
     pl.when(has_prev)(to_prev.wait_send)
     pl.when(has_next)(to_next.wait_send)
-    out0.wait()
-    out1.wait()
 
 
 def body(mode_fields, radius, radial_blocks, axial_blocks, block_columns, interface_nodes):
@@ -302,7 +296,7 @@
         kernel,
         out_shape=[jax.ShapeDtypeStruct((3 * 2 * M, TILE), f32)] * 2,
         in_specs=[anywhere] * 8,
-        out_specs=[anywhere] * 2,
+        out_specs=[pl.BlockSpec(memory_space=pltpu.VMEM)] * 2,
         scratch_shapes=[
             pltpu.VMEM((12, 16, HALF, 2, TILE), bf),
             pltpu.VMEM((12, THETA, TILE), f32),
@@ -314,8 +308,6 @@
             pltpu.VMEM((2 * HALO // TILE, 4, ROWS, TILE), bf),
             pltpu.VMEM((2, EXT // BLK, 4 * ROWS, TILE), bf),
             pltpu.VMEM((tiles, 3, ROWS, TILE), f32),
-            pltpu.VMEM((3 * 2 * M, TILE), f32),
-            pltpu.VMEM((3 * 2 * M, TILE), f32),
             pltpu.VMEM((DEPTH, NODES), bf),
             pltpu.VMEM((DEPTH, NODES), bf),
             pltpu.VMEM((THETA, 2 * M), bf),
@@ -323,15 +315,17 @@
             pltpu.VMEM((2, HALO), jnp.int32),
             pltpu.VMEM((tiles, TILE), f32),
             pltpu.SMEM((NNZB, NODES // BLK), jnp.int32),
-            dma((8,)), dma((2,)),
+            dma((8,)),
             dma((2, 15)), dma((2, 15)), dma((2, 15)), dma((2, 15)), dma((2,)), dma((2,)),
         ],
         compiler_params=pltpu.CompilerParams(
-            collective_id=0, has_side_effects=True, vmem_limit_bytes=56 * 1024 * 1024
+            collective_id=0, has_side_effects=True, vmem_limit_bytes=40 * 1024 * 1024
         ),
     )(
-        mode_fields, inv, fwd, interface_nodes, radius.reshape(tiles, TILE),
-        radial_blocks.reshape(NNZB * BLK, NODES), axial_blocks.reshape(NNZB * BLK, NODES), block_columns.T,
+        *(pltpu.with_memory_space_constraint(a, pltpu.HBM) for a in (
+            mode_fields, inv, fwd, interface_nodes, radius.reshape(tiles, TILE),
+            radial_blocks.reshape(NNZB * BLK, NODES), axial_blocks.reshape(NNZB * BLK, NODES), block_columns.T,
+        ))
     )
 
     def whole(a):

time: 84.9 us -> 79.9 us (0.941)
  the two profiles are of different devices: /device:TPU:8 before, /device:TPU:16 now
where the time goes in v3:
time: 79.9 us; the launch traced here: 79.8 us
  Pallas kernels  77.7 us (97%)
  local copies, waits for them, and re-layouts  1.49 us (2%)
    pallas_call x1, Pallas kernels, body(): pl.pallas_call(kernel, out_shape=[jax.ShapeDtypeStruct((3 * 2 * M, TILE),...  77.7 us

profile of v3, /device:TPU:16, one launch (start us, length us, event | category | flops | bytes accessed | tf_op | source)
XLA Modules:
  0.0 79.8 jit_solution(4995463877432154382)
XLA Ops:
  0.6 77.7 %shard_map.95 = (f32[768,128]{1,0:T(8,128)S(1)}, f32[768,128]{1,0:T(8,128)S(1)}) custom-call(bf16[12,8,2,2048]{3,2,1,0:T(2,128)(2,1)} %x.1, bf16[256,256]{1,0:T(8,128)(2,1)} %constant.4.clone.inv, bf16[256,256]{1,0:T(8,128)(2,1)} %constant.5.clone.fwd, s32[2,256]{1,0:T(2,128)} %nodes.1, f32[16,128]{1,0:T(8,128)} %bitcast.18, bf16[320,2048]{1,0:T(8,128)(2,1)} %bitcast.16, ...), custom_call_target="tpu_custom_call" | custom-call | tf_op jit(solution)/shard_map/pallas_call | solution.py:295
  78.3 0.7 copy.14
  79.0 0.7 copy.15

commit v4 on v3

--- a/solution.py
+++ b/solution.py
@@ -90,16 +90,27 @@
         c.start()
     pl.semaphore_wait(bar, 15 + has_prev.astype(jnp.int32) + has_next.astype(jnp.int32))
 
-    first = []
-    for h in range(2):
+    def over(h, dx, dz):
         part = pl.ds(6 * h, 6)
-        for i, t in enumerate(peers):
-            c = pltpu.make_async_remote_copy(
-                x.at[part, :, :, columns(t)], recv.at[part, me], s1.at[h, i], r1.at[h, i],
-                device_id={"mode": t}, device_id_type=MESH,
-            )
-            c.start()
-            first.append(c)
+        t = lax.rem(mx + dx, 4) * 4 + lax.rem(mz + dz, 4)
+        return pltpu.make_async_remote_copy(
+            x.at[part, :, :, columns(t)], recv.at[part, me], s1.at[h, 4 * dz + dx], r1.at[h, 4 * dz + dx],
+            device_id={"mode": t}, device_id_type=MESH,
+        )
+
+    def serve(copy, *order):
+        for tz in order:
+            dz = lax.rem(tz - mz + 4, 4)
+            for dx in range(4):
+                if dx:
+                    copy(dx, dz).start()
+                else:
+                    pl.when(dz != 0)(lambda: copy(0, dz).start())
+
+    first = [over(h, dx, dz) for h in range(2) for dx, dz in PEERS]
+    for copy in first[0:15]:
+        copy.start()
+    serve(functools.partial(over, 1), 2, 1, 3, 0)
 
     loads[0].wait()
 
@@ -135,17 +146,17 @@
             else:
                 send[k] = dot(fwdv[...], prod[k]).astype(jnp.bfloat16)
 
-    def give(c, n, into, h):
-        out = []
-        for i, t in enumerate(peers):
-            copy = pltpu.make_async_remote_copy(
-                send.at[pl.ds(c, n), rows(t), :], into.at[me], s2.at[h, i], r2.at[h, i],
-                device_id={"mode": t}, device_id_type=MESH,
-            )
-            copy.start()
-            out.append(copy)
+    def back(h, dx, dz):
+        c, n, into = ((0, 4, ext), (4, 3, lor))[h]
+        t = lax.rem(mx + dx, 4) * 4 + lax.rem(mz + dz, 4)
+        return pltpu.make_async_remote_copy(
+            send.at[pl.ds(c, n), rows(t), :], into.at[me], s2.at[h, 4 * dz + dx], r2.at[h, 4 * dz + dx],
+            device_id={"mode": t}, device_id_type=MESH,
+        )
+
+    def keep(h):
+        c, n, into = ((0, 4, ext), (4, 3, lor))[h]
         into[me] = send[c : c + n, rows(me), :]
-        return out
 
     def cross(a, b):
         return [a[1] * b[2] - a[2] * b[1], a[2] * b[0] - a[0] * b[2], a[0] * b[1] - a[1] * b[0]]
@@ -165,7 +176,9 @@
 
     lax.fori_loop(0, THETA // step, early, 0)
     forward(0, 4)
-    second = give(0, 4, ext, 0)
+    second = [back(0, dx, dz) for dx, dz in PEERS]
+    serve(functools.partial(back, 0), 0, 1, 3, 2)
+    keep(0)
     inverse(1)
 
     def late(i, carry):
@@ -178,7 +191,9 @@
 
     lax.fori_loop(0, THETA // step, late, 0)
     forward(4, 3)
-    third = give(4, 3, lor, 1)
+    third = [back(1, dx, dz) for dx, dz in PEERS]
+    serve(functools.partial(back, 1), 0, 1, 3, 2)
+    keep(1)
 
     tiles = NODES // TILE
     side = HALO // TILE
@@ -284,6 +299,18 @@
         c.wait_send()
     pl.when(has_prev)(to_prev.wait_send)
     pl.when(has_next)(to_next.wait_send)
+
+
+def flush(ind, mom, out_ind, out_mom, sem):
+    half = 3 * M
+    copies = []
+    for a, b in ((ind, out_ind), (mom, out_mom)):
+        for part in (pl.ds(0, half), pl.ds(half, half)):
+            c = pltpu.make_async_copy(a.at[part, :], b.at[part, :], sem.at[len(copies)])
+            c.start()
+            copies.append(c)
+    for c in copies:
+        c.wait()
 
 
 def body(mode_fields, radius, radial_blocks, axial_blocks, block_columns, interface_nodes):
@@ -316,7 +343,7 @@
             pltpu.VMEM((tiles, TILE), f32),
             pltpu.SMEM((NNZB, NODES // BLK), jnp.int32),
             dma((8,)),
-            dma((2, 15)), dma((2, 15)), dma((2, 15)), dma((2, 15)), dma((2,)), dma((2,)),
+            dma((2, 16)), dma((2, 16)), dma((2, 16)), dma((2, 16)), dma((2,)), dma((2,)),
         ],
         compiler_params=pltpu.CompilerParams(
             collective_id=0, has_side_effects=True, vmem_limit_bytes=40 * 1024 * 1024
@@ -328,6 +355,15 @@
         ))
     )
 
+    ind, mom = pl.pallas_call(
+        flush,
+        out_shape=[jax.ShapeDtypeStruct((3 * 2 * M, TILE), f32)] * 2,
+        in_specs=[pl.BlockSpec(memory_space=pltpu.VMEM)] * 2,
+        out_specs=[anywhere] * 2,
+        scratch_shapes=[dma((4,))],
+        compiler_params=pltpu.CompilerParams(vmem_limit_bytes=8 * 1024 * 1024),
+    )(ind, mom)
+
     def whole(a):
         a = a.reshape(3, HALF, tiles, 2, TILE)
         return a.transpose(0, 1, 3, 2, 4).reshape(3, HALF, 2, NODES)

time: 79.9 us -> 79.3 us (level)
  the two profiles are of different devices: /device:TPU:16 before, /device:TPU:26 now
where the time goes in v4:
time: 79.3 us; the launch traced here: 79.1 us
  Pallas kernels  78.5 us (99%)
    pallas_call x1, Pallas kernels, body(): pl.pallas_call(kernel, out_shape=[jax.ShapeDtypeStruct((3 * 2 * M, TILE),...  77.6 us

profile of v4, /device:TPU:26, one launch (start us, length us, event | category | flops | bytes accessed | tf_op | source)
XLA Modules:
  0.0 79.1 jit_solution(15168419025640419780)
XLA Ops:
  0.6 77.6 %shard_map.95 = (f32[768,128]{1,0:T(8,128)S(1)}, f32[768,128]{1,0:T(8,128)S(1)}) custom-call(bf16[12,8,2,2048]{3,2,1,0:T(2,128)(2,1)} %x.1, bf16[256,256]{1,0:T(8,128)(2,1)} %constant.4.clone.inv, bf16[256,256]{1,0:T(8,128)(2,1)} %constant.5.clone.fwd, s32[2,256]{1,0:T(2,128)} %nodes.1, f32[16,128]{1,0:T(8,128)} %bitcast.16, bf16[320,2048]{1,0:T(8,128)(2,1)} %bitcast.14, ...), custom_call_target="tpu_custom_call" | custom-call | tf_op jit(solution)/shard_map/pallas_call | solution.py:322
  78.2 0.9 %shard_map.96 = (f32[768,128]{1,0:T(8,128)}, f32[768,128]{1,0:T(8,128)}) custom-call(f32[768,128]{1,0:T(8,128)S(1)} %get-tuple-element.6.ind, f32[768,128]{1,0:T(8,128)S(1)} %get-tuple-element.7.mom), custom_call_target="tpu_custom_call" | custom-call | tf_op jit(solution)/shard_map/pallas_call | solution.py:358

commit v5 on v4

--- a/solution.py
+++ b/solution.py
@@ -284,7 +284,7 @@
         rest[j, 2] = part(along_z, 3)
         return carry
 
-    lax.fori_loop(0, tiles, derive, 0, unroll=4)
+    lax.fori_loop(0, tiles, derive, 0, unroll=8)
 
     for c in third:
         c.wait_recv()

time: 79.3 us -> 79 us (level)
  no operation moved by 1% of the time
where the time goes in v5:
time: 79 us; the launch traced here: 78.9 us
  Pallas kernels  78.2 us (99%)
    pallas_call x1, Pallas kernels, body(): pl.pallas_call(kernel, out_shape=[jax.ShapeDtypeStruct((3 * 2 * M, TILE),...  77.3 us

profile of v5, /device:TPU:26, one launch (start us, length us, event | category | flops | bytes accessed | tf_op | source)
XLA Modules:
  0.0 78.9 jit_solution(3521397769151297057)
XLA Ops:
  0.6 77.3 %shard_map.95 = (f32[768,128]{1,0:T(8,128)S(1)}, f32[768,128]{1,0:T(8,128)S(1)}) custom-call(bf16[12,8,2,2048]{3,2,1,0:T(2,128)(2,1)} %x.1, bf16[256,256]{1,0:T(8,128)(2,1)} %constant.4.clone.inv, bf16[256,256]{1,0:T(8,128)(2,1)} %constant.5.clone.fwd, s32[2,256]{1,0:T(2,128)} %nodes.1, f32[16,128]{1,0:T(8,128)} %bitcast.16, bf16[320,2048]{1,0:T(8,128)(2,1)} %bitcast.14, ...), custom_call_target="tpu_custom_call" | custom-call | tf_op jit(solution)/shard_map/pallas_call | solution.py:322
  78.0 0.9 %shard_map.96 = (f32[768,128]{1,0:T(8,128)}, f32[768,128]{1,0:T(8,128)}) custom-call(f32[768,128]{1,0:T(8,128)S(1)} %get-tuple-element.6.ind, f32[768,128]{1,0:T(8,128)S(1)} %get-tuple-element.7.mom), custom_call_target="tpu_custom_call" | custom-call | tf_op jit(solution)/shard_map/pallas_call | solution.py:358

commit v6 on v5

--- a/solution.py
+++ b/solution.py
@@ -321,7 +321,7 @@
     tiles = NODES // TILE
     ind, mom = pl.pallas_call(
         kernel,
-        out_shape=[jax.ShapeDtypeStruct((3 * 2 * M, TILE), f32)] * 2,
+        out_shape=[jax.ShapeDtypeStruct((3 * 2 * M + 32, TILE), f32)] * 2,
         in_specs=[anywhere] * 8,
         out_specs=[pl.BlockSpec(memory_space=pltpu.VMEM)] * 2,
         scratch_shapes=[

time: 79 us -> 79 us (level)
  no operation moved by 1% of the time
where the time goes in v6:
time: 79 us; the launch traced here: 78.9 us
  Pallas kernels  78.2 us (99%)
    pallas_call x1, Pallas kernels, body(): pl.pallas_call(kernel, out_shape=[jax.ShapeDtypeStruct((3 * 2 * M + 32, T...  77.3 us

profile of v6, /device:TPU:26, one launch (start us, length us, event | category | flops | bytes accessed | tf_op | source)
XLA Modules:
  0.0 78.9 jit_solution(7081064525322679713)
XLA Ops:
  0.6 77.3 %shard_map.95 = (f32[800,128]{1,0:T(8,128)S(1)}, f32[800,128]{1,0:T(8,128)S(1)}) custom-call(bf16[12,8,2,2048]{3,2,1,0:T(2,128)(2,1)} %x.1, bf16[256,256]{1,0:T(8,128)(2,1)} %constant.4.clone.inv, bf16[256,256]{1,0:T(8,128)(2,1)} %constant.5.clone.fwd, s32[2,256]{1,0:T(2,128)} %nodes.1, f32[16,128]{1,0:T(8,128)} %bitcast.16, bf16[320,2048]{1,0:T(8,128)(2,1)} %bitcast.14, ...), custom_call_target="tpu_custom_call" | custom-call | tf_op jit(solution)/shard_map/pallas_call | solution.py:322
  78.0 0.9 %shard_map.96 = (f32[768,128]{1,0:T(8,128)}, f32[768,128]{1,0:T(8,128)}) custom-call(f32[800,128]{1,0:T(8,128)S(1)} %get-tuple-element.6.ind, f32[800,128]{1,0:T(8,128)S(1)} %get-tuple-element.7.mom), custom_call_target="tpu_custom_call" | custom-call | tf_op jit(solution)/shard_map/pallas_call | solution.py:358
